TPU v7x, 256 devices: a whole 4x4x8 slice. The times are simulated.
256 devices in a mesh: head: 8 (over y, core), seq: 32 (over z, x).
Axes of the slice: x: 4, y: 4, z: 8, core: 2. Of those that a mesh axis runs over, the one named last changes fastest.
Arguments:
- queries: bfloat16 [32768, 2048], P('seq', 'head'), may hold values from -4 to 4
- keys: bfloat16 [32768, 2048], P('seq', 'head'), may hold values from -4 to 4
- values: bfloat16 [32768, 4096], P('seq', 'head'), may hold values from -6 to 6
- input_gate: float32 [32768, 8], P('seq', 'head'), may hold values from -4 to 4
- forget_gate: float32 [32768, 8], P('seq', 'head')
- out_weight: bfloat16 [4096, 4096], P('head', 'seq'), may hold values from -0.09375 to 0.09375
Outputs:
- mixed: bfloat16 [32768, 4096], P('seq', 'head')
All inputs are finite; a program needn't handle non-finite values.
Results may differ from a plain program's by a relative error of at most 0.019.
Values may be sent and summed in bfloat16 or wider, within the bound.
A program may use at most 128 MiB of HBM per device.

v0:
```python
import jax
import jax.numpy as jnp
from jax import lax
from jax.sharding import PartitionSpec as P

WINDOW = 1024
PRECISE = lax.Precision.HIGHEST
VERY_NEGATIVE = -1e30


def from_behind(block, axis, distance):
    devices = range(lax.axis_size(axis))
    route = [(i - distance, i) for i in devices if i - distance in devices]
    return lax.ppermute(block, axis, route)


def entering(part, axis, combine, identity):
    place = lax.axis_index(axis)
    gathered = jax.tree.map(lambda a: lax.all_gather(a, axis), part)
    state = jax.tree.map(lambda a, e: jnp.zeros_like(a) + jnp.asarray(e, a.dtype), part, identity)

    def one(hop, state):
        return combine(
            state, jax.tree.map(lambda a: lax.dynamic_index_in_dim(a, hop, 0, False), gathered)
        )

    return lax.fori_loop(0, place, one, state)


def memory_block(query_rows, key_rows, value_rows, gate_keys, cum_query, cum_key, carry_state):
    mem_c, mem_n, mem_m = carry_state
    key_scale = query_rows.shape[-1] ** (-0.5)
    scores = jnp.dot(query_rows, key_rows.T, preferred_element_type=jnp.float32) * key_scale
    query_index = jnp.arange(query_rows.shape[0], dtype=jnp.int32)
    key_index = jnp.arange(key_rows.shape[0], dtype=jnp.int32)
    causal = key_index[None, :] <= query_index[:, None]
    log_decay = jnp.where(
        causal, cum_query[:, None] - cum_key[None, :] + gate_keys[None, :], VERY_NEGATIVE
    )
    carry_log = cum_query + mem_m
    mem_max = jnp.maximum(jnp.max(log_decay, axis=1), carry_log)
    decays = jnp.where(causal, jnp.exp(log_decay - mem_max[:, None]), 0.0)
    weighted = decays * scores
    carry_scale = jnp.exp(carry_log - mem_max)
    query_full = query_rows.astype(jnp.float32) * key_scale
    numerator = jnp.dot(
        weighted.astype(jnp.bfloat16), value_rows, preferred_element_type=jnp.float32
    )
    numerator = numerator + carry_scale[:, None] * jnp.dot(query_full, mem_c, precision=PRECISE)
    denominator = jnp.sum(weighted, axis=1) + carry_scale * jnp.dot(
        query_full, mem_n, precision=PRECISE
    )
    return (numerator, denominator, mem_max)


def window_block(query_rows, key_window, value_window, query_pos, key_pos, mem_max):
    key_scale = query_rows.shape[-1] ** (-0.5)
    scores = jnp.dot(query_rows, key_window.T, preferred_element_type=jnp.float32) * key_scale
    visible = (
        (key_pos[None, :] <= query_pos[:, None])
        & (key_pos[None, :] > query_pos[:, None] - WINDOW)
        & (key_pos[None, :] >= 0)
    )
    top_score = jnp.max(jnp.where(visible, scores, VERY_NEGATIVE), axis=1)
    joint_max = jnp.maximum(top_score, mem_max)
    weights = jnp.where(visible, jnp.exp(scores - joint_max[:, None]), 0.0)
    numerator = jnp.dot(
        weights.astype(jnp.bfloat16), value_window, preferred_element_type=jnp.float32
    )
    return (numerator, jnp.sum(weights, axis=1), joint_max)


def joint_output(window, memory):
    win_num, win_den, joint_max = window
    mem_num, mem_den, mem_max = memory
    lifted = jnp.exp(mem_max - joint_max)
    bottom = win_den + lifted * jnp.maximum(jnp.abs(mem_den), 1.0)
    return ((win_num + lifted[:, None] * mem_num) / bottom[:, None]).astype(jnp.bfloat16)


def span_summary(key_rows, value_rows, gate_keys, cum_key):
    total_decay = cum_key[-1]
    log_weight = total_decay - cum_key + gate_keys
    new_max = jnp.max(log_weight)
    scaled_keys = key_rows.astype(jnp.float32) * jnp.exp(log_weight - new_max)[:, None]
    mem_c = jnp.dot(scaled_keys.T, value_rows.astype(jnp.float32), precision=PRECISE)
    return (mem_c, jnp.sum(scaled_keys, axis=0), new_max, total_decay)


def merge_states(older, newer):
    lifted = newer[3] + older[2]
    new_max = jnp.maximum(lifted, newer[2])
    old_weight = jnp.exp(lifted - new_max)
    new_weight = jnp.exp(newer[2] - new_max)
    mem_c = old_weight[..., None, None] * older[0] + new_weight[..., None, None] * newer[0]
    mem_n = old_weight[..., None] * older[1] + new_weight[..., None] * newer[1]
    return (mem_c, mem_n, new_max, older[3] + newer[3])


def split_heads(matrix, head_count):
    return matrix.reshape(matrix.shape[0], head_count, matrix.shape[1] // head_count).transpose(
        1, 0, 2
    )


def local(queries, keys, values, input_gate, forget_gate, out_weight):
    row_count = queries.shape[0]
    local_heads = input_gate.shape[1]
    tail_pair = (keys, values)
    pieces = [from_behind((tail_pair[0], tail_pair[1]), "seq", 1)]
    ext_keys = jnp.concatenate([entry[0] for entry in pieces[::-1]] + [keys], axis=0)
    ext_values = jnp.concatenate([entry[1] for entry in pieces[::-1]] + [values], axis=0)
    query_heads = split_heads(queries, local_heads)
    key_heads = split_heads(keys, local_heads)
    value_heads = split_heads(values, local_heads)
    ext_key_heads = split_heads(ext_keys, local_heads)
    ext_value_heads = split_heads(ext_values, local_heads)
    gate_heads = input_gate.T
    cum_heads = jnp.cumsum(jax.nn.log_sigmoid(forget_gate.T), axis=1)
    summaries = jax.vmap(span_summary)(key_heads, value_heads, gate_heads, cum_heads)
    identity = (
        jnp.zeros_like(summaries[0]),
        jnp.zeros_like(summaries[1]),
        jnp.full_like(summaries[2], VERY_NEGATIVE),
        jnp.zeros_like(summaries[3]),
    )
    carried = entering(summaries, "seq", merge_states, identity)
    base_pos = lax.axis_index("seq") * row_count
    block_rows = min(row_count, 512)

    def head_output(
        query_all, key_all, value_all, key_ext, value_ext, gate_keys, cum_gate, mem_c, mem_n, mem_m
    ):
        results = []
        state = (mem_c, mem_n, mem_m, jnp.zeros_like(mem_m))
        for block_index in range(row_count // block_rows):
            first_row = block_index * block_rows
            last_row = first_row + block_rows
            query_rows = query_all[first_row:last_row]
            key_rows = key_all[first_row:last_row]
            value_rows = value_all[first_row:last_row]
            gate_rows = gate_keys[first_row:last_row]
            local_cum = cum_gate[first_row:last_row]
            if first_row > 0:
                local_cum = local_cum - cum_gate[first_row - 1]
            memory = memory_block(
                query_rows, key_rows, value_rows, gate_rows, local_cum, local_cum, state[:3]
            )
            key_window = key_ext[first_row : last_row + WINDOW]
            value_window = value_ext[first_row : last_row + WINDOW]
            query_pos = base_pos + first_row + jnp.arange(block_rows, dtype=jnp.int32)
            key_pos = (
                base_pos + first_row - WINDOW + jnp.arange(WINDOW + block_rows, dtype=jnp.int32)
            )
            window = window_block(
                query_rows, key_window, value_window, query_pos, key_pos, memory[2]
            )
            results.append(joint_output(window, memory))
            if last_row < row_count:
                state = merge_states(
                    state, span_summary(key_rows, value_rows, gate_rows, local_cum)
                )
        return jnp.concatenate(results, axis=0)

    hidden_heads = jax.vmap(head_output)(
        query_heads,
        key_heads,
        value_heads,
        ext_key_heads,
        ext_value_heads,
        gate_heads,
        cum_heads,
        carried[0],
        carried[1],
        carried[2],
    )
    hidden = hidden_heads.transpose(1, 0, 2).reshape(row_count, local_heads * hidden_heads.shape[2])
    partial_terms = jnp.dot(
        hidden,
        lax.all_gather(out_weight, "seq", axis=1, tiled=True),
        preferred_element_type=jnp.float32,
    )
    mixed = lax.psum_scatter(
        partial_terms.astype(jnp.bfloat16), "head", scatter_dimension=1, tiled=True
    )
    return mixed


def solution(mesh):
    placed = (
        P("seq", "head"),
        P("seq", "head"),
        P("seq", "head"),
        P("seq", "head"),
        P("seq", "head"),
        P("head", "seq"),
    )
    return jax.shard_map(
        local, mesh=mesh, in_specs=placed, out_specs=P("seq", "head"), check_vma=False
    )
```

profile of v0, /device:TPU:1, one launch (start us, length us, event | category | flops | bytes accessed | tf_op | source)
XLA Modules:
  0.0 400.4 jit_solution(119145561673392502)
XLA Ops:
  6.5 0.8 neg.43
  7.3 0.3 reduce-window.6
  7.6 0.2 slice_reduce_fusion
  7.8 0.2 reduce-window.9
  8.0 0.1 broadcast.348
  8.1 0.7 fusion.103
  8.7 1.9 add_reduce_fusion
  10.7 2.0 fusion.89
  12.6 3.5 fusion.42
  16.2 0.0 all-gather.6.cloned.1.call-start
  16.3 4.0 collective-permute-start
  20.2 3.2 collective-permute-start.1
  23.4 0.0 all-gather.6.cloned.1.call-update
  23.4 0.0 reduce-scatter.2.cloned.1.call-start
  23.6 0.7 slice.80
  24.2 1.2 dynamic-slice
  25.5 1.2 bitcast_dynamic-update-slice_fusion
  26.7 1.3 dynamic-update-slice.1
  28.0 97.5 %all-reduce.2 = (f32[32]{0:T(128)S(1)}, f32[32]{0:T(128)S(1)}) all-reduce(f32[32]{0:T(128)S(1)} %bitcast_dynamic-update-slice_fusion, f32[32]{0:T(128)S(1)} %dynamic-update-slice.1), channel_id=1, replica_groups=mesh['head'=8,'seq'=32] {'seq'}, use_global_device_ids=true, to_apply=%add | all-reduce | flops 64 | bytes 512
  125.5 0.2 fusion.41
  125.7 0.3 select_reduce_fusion.3
  126.0 41.6 %all-gather.2 = f32[32,1,256]{2,1,0:T(1,128)S(1)} all-gather(f32[1,1,256]{2,1,0:T(1,128)S(1)} %bitcast.249), channel_id=3, replica_groups=mesh['head'=8,'seq'=32] {'seq'}, dimensions={0}, use_global_device_ids=true | all-gather | bytes 33792 | tf_op jit(solution)/shard_map/all_gather | solution.py:19
  167.6 0.1 maximum_bitcast_fusion.1
  167.7 3.0 select_reduce_fusion.1
  170.8 3.0 select_reduce_fusion
  173.8 1.4 maximum_bitcast_fusion
  175.3 0.2 while.16
  176.4 0.8 subtract_exponential_fusion.4
  177.2 1.3 fusion.102
  179.8 0.7 subtract_exponential_fusion
  180.5 0.1 fusion.60
  180.6 0.3 select_reduce_fusion.2
  180.9 0.8 fusion.28
  181.7 0.4 fusion.105
  182.2 1.5 fusion.2
  183.7 0.6 fusion.38
  184.3 0.4 fusion.104
  184.7 1.5 fusion.4
  186.2 0.6 fusion.33
  186.8 0.5 fusion.62
  187.3 0.5 fusion.53
  187.8 1.1 fusion.17
  188.9 1.1 fusion.15
  190.0 1.9 fusion.50
  191.9 1.8 fusion.45
  193.7 60.6 %all-gather.6.cloned.1.call-done = bf16[512,4096]{1,0:T(8,128)(2,1)} async-done(((bf16[512,128]{1,0:T(8,128)(2,1)}), bf16[512,4096]{1,0:T(8,128)(2,1)}) %all-gather.6.cloned.1.call-update) | async-done | bytes 4194320 | tf_op jit(solution)/shard_map/all_gather | solution.py:180
  254.3 9.6 %convolution_convert_fusion = bf16[1024,4096]{1,0:T(8,128)(2,1)} fusion(bf16[512,4096]{1,0:T(8,128)(2,1)} %all-gather.6.cloned.1.call-done, bf16[1,512,512]{2,1,0:T(8,128)(2,1)S(1)} %fusion.45, bf16[1,512,512]{2,1,0:T(8,128)(2,1)S(1)} %fusion.50), kind=kOutput, calls=%fused_computation.4 | convolution fusion | flops 4301258752 | bytes 13631488 | tf_op jit(solution)/shard_map/dot_general | solution.py:178
  263.9 129.9 %reduce-scatter.2.cloned.1.call-done = bf16[1024,512]{1,0:T(8,128)(2,1)} async-done(((bf16[1024,4096]{1,0:T(8,128)(2,1)}), bf16[1024,512]{1,0:T(8,128)(2,1)}) %reduce-scatter.2.cloned.1.call-update) | async-done | bytes 1048592 | tf_op jit(solution)/shard_map/reduce_scatter | solution.py:183
  (41 shorter events, 0.2 us)
Async XLA Ops:
  6.5 119.0 %copy-start.1 = (bf16[1024,256]{1,0:T(8,128)(2,1)S(1)}, bf16[1024,256]{1,0:T(8,128)(2,1)}, u32[]{:S(2)}) copy-start(bf16[1024,256]{1,0:T(8,128)(2,1)} %param.9) | copy-start | bytes 1572868
  6.5 161.2 %copy-start.5 = (bf16[1024,256]{1,0:T(8,128)(2,1)S(1)}, bf16[1024,256]{1,0:T(8,128)(2,1)}, u32[]{:S(2)}) copy-start(bf16[1024,256]{1,0:T(8,128)(2,1)} %param.8) | copy-start | bytes 1572868
  6.5 168.7 %all-gather.8.cloned.1.call-start = ((), (), s32[]{:S(2)}) async-start(), calls=%async_computation.3 | async-start | bytes 17301504 | tf_op jit(solution)/shard_map/all_gather | solution.py:19
  16.2 238.1 %all-gather.6.cloned.1.call-start = ((), (), s32[]{:S(2)}) async-start(), calls=%async_computation.1 | async-start | bytes 4325376 | tf_op jit(solution)/shard_map/all_gather | solution.py:180
  16.3 151.4 %collective-permute-start = (bf16[1024,256]{1,0:T(8,128)(2,1)}, bf16[1024,256]{1,0:T(8,128)(2,1)S(1)}, u32[]{:S(2)}, u32[]{:S(2)}) collective-permute-start(bf16[1024,256]{1,0:T(8,128)(2,1)} %param.9), channel_id=1, source_target_pairs={{0,1},{1,2},{2,3},{3,4},{4,5},{5,6},{6,7},{7,8},{8,9},{9,10},{10,1... | collective-permute-start | bytes 1572872 | tf_op jit(solution)/shard_map/ppermute | solution.py:14
  20.2 153.6 %collective-permute-start.1 = (bf16[1024,512]{1,0:T(8,128)(2,1)}, bf16[1024,512]{1,0:T(8,128)(2,1)S(1)}, u32[]{:S(2)}, u32[]{:S(2)}) collective-permute-start(bf16[1024,512]{1,0:T(8,128)(2,1)} %param.10), channel_id=1, source_target_pairs={{0,1},{1,2},{2,3},{3,4},{4,5},{5,6},{6,7},{7,8},{8,9},{9,10},{10,1... | collective-permute-start | bytes 3145736 | tf_op jit(solution)/shard_map/ppermute | solution.py:14
  23.4 370.4 %reduce-scatter.2.cloned.1.call-start = ((), (), s32[]{:S(2)}) async-start(), calls=%async_computation.2 | async-start | bytes 9437184 | tf_op jit(solution)/shard_map/reduce_scatter | solution.py:183
  167.7 3.0 copy-start.6
  170.8 3.0 copy-start
  175.3 1.9 copy-start.8
  175.3 6.4 %copy-start.7 = (bf16[1024,256]{1,0:T(8,128)(2,1)S(1)}, bf16[1024,256]{1,0:T(8,128)(2,1)}, u32[]{:S(2)}) copy-start(bf16[1024,256]{1,0:T(8,128)(2,1)} %param.8) | copy-start | bytes 1572868
  175.5 6.6 %copy-start.3 = (f32[512,1536]{0,1:T(8,128)S(1)}, f32[512,1536]{0,1:T(8,128)}, u32[]{:S(2)}) copy-start(f32[512,1536]{0,1:T(8,128)} %get-tuple-element.156) | copy-start | bytes 9437188
  182.2 2.5 copy-start.2
  187.8 2.3 copy-start.4
Sparse Core Ops, SparseCore 0:
  16.3 158.3 all-gather.7
  177.2 77.0 all-gather.5
  264.0 129.7 reduce-scatter.1
where the time goes:
time: 403 us; the launch traced here: 400 us
  waiting for transfers between devices  191 us (47%)
  blocking collectives  139 us (34%)
  matrix products  28.8 us (7%)
  between operations  15.6 us (4%)
  other arithmetic  13.3 us (3%)
  starting transfers between devices  7.22 us (2%)
  local copies, waits for them, and re-layouts  5.45 us (1%)
    reduce_scatter x1, waiting for transfers between devices, local(): lax.psum_scatter(partial_terms.astype(jnp.bfloat16), 'head', scatter_dime...  130 us
    unnamed x1, blocking collectives  97.5 us
    all_gather x1, waiting for transfers between devices, local(): lax.all_gather(out_weight, 'seq', axis=1, tiled=True)  60.6 us
    all_gather x1, blocking collectives, entering(): gathered = jax.tree.map(lambda a: lax.all_gather(a, axis), part)  41.6 us
    dot_general x1, matrix products, local(): jnp.dot(hidden, lax.all_gather(out_weight, 'seq', axis=1, tiled=True), pr...  9.6 us
  transfers between devices with their start and end apart: 5, of which 2 were waited for; matrix products, arithmetic and copies ran while one was open for 7% of the time, Pallas kernels for 0%

commit v1 on v0

--- a/solution.py
+++ b/solution.py
@@ -104,6 +104,19 @@
 
 
 def local(queries, keys, values, input_gate, forget_gate, out_weight):
+
+    def see_heaps_on(payload, bus_axis):
+        carry = jnp.concatenate(
+            lax.all_to_all(
+                jnp.stack(lax.psum(1, axis_name=bus_axis) * [payload], axis=0),
+                concat_axis=0,
+                split_axis=0,
+                axis_name=bus_axis,
+            ),
+            1,
+        )
+        return carry
+
     row_count = queries.shape[0]
     local_heads = input_gate.shape[1]
     tail_pair = (keys, values)
@@ -176,9 +189,7 @@
     )
     hidden = hidden_heads.transpose(1, 0, 2).reshape(row_count, local_heads * hidden_heads.shape[2])
     partial_terms = jnp.dot(
-        hidden,
-        lax.all_gather(out_weight, "seq", axis=1, tiled=True),
-        preferred_element_type=jnp.float32,
+        hidden, see_heaps_on(out_weight, "seq"), preferred_element_type=jnp.float32
     )
     mixed = lax.psum_scatter(
         partial_terms.astype(jnp.bfloat16), "head", scatter_dimension=1, tiled=True

time: 403 us -> 515 us (1.28)
  blocking collectives: 139 us -> 234 us
  starting transfers between devices: 7.22 us -> 17.6 us
    unnamed x1, blocking collectives: 97.5 us -> 202 us
    reduce_scatter x1, waiting for transfers between devices: 130 us -> 195 us  [local(): lax.psum_scatter(partial_terms.astype(jnp.bfloat16), 'head', scatter_dime...]
    all_gather x1 -> x0, waiting for transfers between devices: 60.6 us -> none  [local(): lax.all_gather(out_weight, 'seq', axis=1, tiled=True)]
    all_to_all x0 -> x1, starting transfers between devices: none -> 10.4 us  [see_heaps_on(): lax.all_to_all(jnp.stack(lax.psum(1, axis_name=bus_axis) * [payload], axi...]
    all_gather x1, blocking collectives: 41.6 us -> 32.1 us  [entering(): gathered = jax.tree.map(lambda a: lax.all_gather(a, axis), part)]
  transfers between devices with their start and end apart: 5 -> 5, of which waited for: 2 -> 1; matrix products, arithmetic and copies ran while one was open for 7% -> 6% of each run, Pallas kernels for 0% -> 0%
where the time goes in v1:
time: 515 us; the launch traced here: 513 us
  blocking collectives  234 us (45%)
  waiting for transfers between devices  195 us (38%)
  matrix products  28.8 us (6%)
  starting transfers between devices  17.6 us (3%)
  between operations  16 us (3%)
  other arithmetic  13.2 us (3%)
  local copies, waits for them, and re-layouts  7.67 us (1%)
    unnamed x1, blocking collectives  202 us
    reduce_scatter x1, waiting for transfers between devices, local(): lax.psum_scatter(partial_terms.astype(jnp.bfloat16), 'head', scatter_dime...  195 us
    all_gather x1, blocking collectives, entering(): gathered = jax.tree.map(lambda a: lax.all_gather(a, axis), part)  32.1 us
    all_to_all x1, starting transfers between devices, see_heaps_on(): lax.all_to_all(jnp.stack(lax.psum(1, axis_name=bus_axis) * [payload], axi...  10.4 us
  transfers between devices with their start and end apart: 5, of which 1 were waited for; matrix products, arithmetic and copies ran while one was open for 6% of the time, Pallas kernels for 0%

profile of v1, /device:TPU:1, one launch (start us, length us, event | category | flops | bytes accessed | tf_op | source)
XLA Modules:
  0.0 512.5 jit_solution(3924135511577097506)
XLA Ops:
  6.5 0.7 neg.43
  7.2 0.3 reduce-window.6
  7.5 0.2 slice_reduce_fusion
  7.7 0.2 reduce-window.9
  7.9 0.1 broadcast.350
  8.0 0.7 fusion.103
  8.6 1.9 add_reduce_fusion
  10.6 1.9 fusion.89
  12.5 3.5 fusion.42
  16.1 0.0 all-gather.5.cloned.1.call-update
  16.1 4.0 collective-permute-start
  20.1 3.2 collective-permute-start.1
  23.2 1.0 copy.13
  24.2 2.4 stack.2
  26.7 10.4 %all-to-all-start = ((bf16[32,512,128]{1,2,0:T(8,128)(2,1)}), bf16[32,512,128]{1,2,0:T(8,128)(2,1)}, u32[]{:S(2)}, u32[]{:S(2)}) async-start(bf16[32,512,128]{1,2,0:T(8,128)(2,1)} %stack.2), calls=%async_computation | async-start | bytes 8388608 | tf_op jit(solution)/shard_map/all_to_all | solution.py:110
  37.1 0.0 reduce-scatter.2.cloned.1.call-start
  37.2 0.6 dynamic-slice
  37.9 1.3 bitcast_dynamic-update-slice_fusion
  39.2 1.3 dynamic-update-slice.1
  40.5 202.1 %all-reduce.2 = (f32[32]{0:T(128)S(1)}, f32[32]{0:T(128)S(1)}) all-reduce(f32[32]{0:T(128)S(1)} %bitcast_dynamic-update-slice_fusion, f32[32]{0:T(128)S(1)} %dynamic-update-slice.1), channel_id=1, replica_groups=mesh['head'=8,'seq'=32] {'seq'}, use_global_device_ids=true, to_apply=%add | all-reduce | flops 64 | bytes 512
  242.6 0.2 fusion.41
  242.8 0.3 select_reduce_fusion.3
  243.0 32.1 %all-gather.2 = f32[32,1,256]{2,1,0:T(1,128)S(1)} all-gather(f32[1,1,256]{2,1,0:T(1,128)S(1)} %bitcast.252), channel_id=3, replica_groups=mesh['head'=8,'seq'=32] {'seq'}, dimensions={0}, use_global_device_ids=true | all-gather | bytes 33792 | tf_op jit(solution)/shard_map/all_gather | solution.py:19
  275.1 0.1 maximum_bitcast_fusion.1
  275.2 3.0 select_reduce_fusion.1
  278.2 3.1 select_reduce_fusion
  281.3 1.5 maximum_bitcast_fusion
  282.9 0.2 while.16
  283.9 0.8 subtract_exponential_fusion.4
  284.7 1.3 fusion.102
  287.4 0.7 subtract_exponential_fusion
  288.0 0.1 fusion.60
  288.2 0.3 select_reduce_fusion.2
  288.4 0.7 fusion.28
  289.2 0.4 fusion.105
  289.7 1.5 fusion.2
  291.2 0.6 fusion.38
  291.8 0.4 fusion.104
  292.2 1.5 fusion.4
  293.7 0.6 fusion.33
  294.3 0.5 fusion.62
  294.8 0.5 fusion.53
  295.3 1.1 fusion.17
  296.4 1.1 fusion.15
  297.5 1.8 fusion.50
  299.3 1.8 fusion.45
  301.1 9.6 %convolution_convert_fusion = bf16[1024,4096]{1,0:T(8,128)(2,1)} fusion(bf16[512,4096]{0,1:T(8,128)(2,1)} %bitcast.87, bf16[1,512,512]{2,1,0:T(8,128)(2,1)S(1)} %fusion.45, bf16[1,512,512]{2,1,0:T(8,128)(2,1)S(1)} %fusion.50), kind=kOutput, calls=%fused_computation.4 | convolution fusion | flops 4301258752 | bytes 13631488 | tf_op jit(solution)/shard_map/dot_general | solution.py:191
  310.8 194.9 %reduce-scatter.2.cloned.1.call-done = bf16[1024,512]{1,0:T(8,128)(2,1)} async-done(((bf16[1024,4096]{1,0:T(8,128)(2,1)}), bf16[1024,512]{1,0:T(8,128)(2,1)}) %reduce-scatter.2.cloned.1.call-update) | async-done | bytes 1048592 | tf_op jit(solution)/shard_map/reduce_scatter | solution.py:194
  (44 shorter events, 0.2 us)
Async XLA Ops:
  6.5 276.3 %all-gather.5.cloned.1.call-start = ((), (), s32[]{:S(2)}) async-start(), calls=%async_computation.3 | async-start | bytes 17301504 | tf_op jit(solution)/shard_map/all_gather | solution.py:19
  16.1 259.0 %collective-permute-start = (bf16[1024,256]{1,0:T(8,128)(2,1)}, bf16[1024,256]{1,0:T(8,128)(2,1)S(1)}, u32[]{:S(2)}, u32[]{:S(2)}) collective-permute-start(bf16[1024,256]{1,0:T(8,128)(2,1)} %param.9), channel_id=1, source_target_pairs={{0,1},{1,2},{2,3},{3,4},{4,5},{5,6},{6,7},{7,8},{8,9},{9,10},{10,1... | collective-permute-start | bytes 1572872 | tf_op jit(solution)/shard_map/ppermute | solution.py:14
  20.1 261.3 %collective-permute-start.1 = (bf16[1024,512]{1,0:T(8,128)(2,1)}, bf16[1024,512]{1,0:T(8,128)(2,1)S(1)}, u32[]{:S(2)}, u32[]{:S(2)}) collective-permute-start(bf16[1024,512]{1,0:T(8,128)(2,1)} %param.10), channel_id=1, source_target_pairs={{0,1},{1,2},{2,3},{3,4},{4,5},{5,6},{6,7},{7,8},{8,9},{9,10},{10,1... | collective-permute-start | bytes 3145736 | tf_op jit(solution)/shard_map/ppermute | solution.py:14
  26.7 10.5 %copy-start.8 = (f32[1024,1]{0,1:T(1,128)S(1)}, f32[1024,1]{0,1:T(1,128)}, u32[]{:S(2)}) copy-start(f32[1024,1]{0,1:T(1,128)} %param.11) | copy-start | bytes 12292
  26.7 10.5 %copy-start.9 = (u32[256]{0:T(256)S(1)}, u32[256]{0:T(256)}, u32[]{:S(2)}) copy-start(u32[256]{0:T(256)} %constant.67) | copy-start | bytes 3076
  26.7 215.9 %copy-start.1 = (bf16[1024,256]{1,0:T(8,128)(2,1)S(1)}, bf16[1024,256]{1,0:T(8,128)(2,1)}, u32[]{:S(2)}) copy-start(bf16[1024,256]{1,0:T(8,128)(2,1)} %param.9) | copy-start | bytes 1572868
  26.7 248.5 %copy-start.5 = (bf16[1024,256]{1,0:T(8,128)(2,1)S(1)}, bf16[1024,256]{1,0:T(8,128)(2,1)}, u32[]{:S(2)}) copy-start(bf16[1024,256]{1,0:T(8,128)(2,1)} %param.8) | copy-start | bytes 1572868
  26.7 274.4 %all-to-all-start = ((bf16[32,512,128]{1,2,0:T(8,128)(2,1)}), bf16[32,512,128]{1,2,0:T(8,128)(2,1)}, u32[]{:S(2)}, u32[]{:S(2)}) async-start(bf16[32,512,128]{1,2,0:T(8,128)(2,1)} %stack.2), calls=%async_computation | async-start | bytes 8388608 | tf_op jit(solution)/shard_map/all_to_all | solution.py:110
  37.1 468.5 %reduce-scatter.2.cloned.1.call-start = ((), (), s32[]{:S(2)}) async-start(), calls=%async_computation.2 | async-start | bytes 9437184 | tf_op jit(solution)/shard_map/reduce_scatter | solution.py:194
  275.2 3.0 copy-start.6
  278.2 3.1 copy-start
  282.9 6.4 %copy-start.7 = (bf16[1024,256]{1,0:T(8,128)(2,1)S(1)}, bf16[1024,256]{1,0:T(8,128)(2,1)}, u32[]{:S(2)}) copy-start(bf16[1024,256]{1,0:T(8,128)(2,1)} %param.8) | copy-start | bytes 1572868
  283.1 6.6 %copy-start.3 = (f32[512,1536]{0,1:T(8,128)S(1)}, f32[512,1536]{0,1:T(8,128)}, u32[]{:S(2)}) copy-start(f32[512,1536]{0,1:T(8,128)} %get-tuple-element.156) | copy-start | bytes 9437188
  289.7 2.5 copy-start.2
  295.2 2.2 copy-start.4
Sparse Core Ops, SparseCore 0:
  16.2 219.2 all-gather.4
  310.9 194.7 reduce-scatter.1
